TPU v7x, 256 devices: a whole 4x4x8 slice. The times are simulated.
256 devices in a mesh: modes: 64 (over z_hi, x, y, core), pix: 4 (over z_lo).
Axes of the slice: x: 4, y: 4, z: 8 (z_hi: 2, z_lo: 4; z = z_hi * 4 + z_lo), core: 2. Of those that a mesh axis runs over, the one named last changes fastest.
Arguments:
- pixel_modes: bfloat16 [2048, 98304], P('pix', 'modes'), may hold values from -6 to 6
- weighted_modes: bfloat16 [2048, 98304], P('pix', 'modes'), may hold values from -0.01171875 to 0.01171875
- mode_bins: int32 [98304], replicated, may hold values from 0 to 127
- live_counts: int32 [8, 2], P('pix'), may hold values from 17 to 128
Outputs:
- fisher_tiles: float32 [64, 5, 128, 128], P('modes')
All inputs are finite; a program needn't handle non-finite values.
Results may differ from a plain program's by a relative error of at most 0.0003.
Values may be sent and summed in bfloat16 or wider, within the bound.
No kernel may reach another device: no remote copies, remote signals or barrier semaphores. Data moves between devices by JAX's collectives and lax.ppermute only.
A program may use at most 128 MiB of HBM per device.

v0:
```python
import jax
import jax.numpy as jnp
from jax import lax
from jax.sharding import PartitionSpec as P

NB = 128
ROW_BLOCK = 128
ROUNDS = 5


def from_behind(block, axis, distance):
    devices = range(lax.axis_size(axis))
    route = [((i - distance) % len(devices), i) for i in devices]
    return lax.ppermute(block, axis, route)


def bin_table(bin_ids):
    return (bin_ids[:, None] == jnp.arange(NB, dtype=jnp.int32)[None, :]).astype(jnp.float32)


def bin_tile(flipped, partner_bins, own_table):
    squares = flipped * flipped
    partner_table = bin_table(partner_bins)
    left = lax.dot_general(
        partner_table, squares, (((0,), (0,)), ((), ())), precision=lax.Precision.HIGHEST
    )
    return 0.5 * jnp.dot(left, own_table, precision=lax.Precision.HIGHEST).T


def shards(pixel_modes, weighted_modes, mode_bins, live_counts):
    row_count, col_count = pixel_modes.shape
    groups = lax.axis_size("pix")
    cycle_size = lax.axis_size("modes")
    quarter = col_count // groups
    own_index = lax.axis_index("modes")
    pix_index = lax.axis_index("pix")
    offsets = lax.broadcasted_iota(
        jnp.int32, (live_counts.shape[0], live_counts.shape[1], ROW_BLOCK), 2
    )
    live_rows = (offsets < live_counts[:, :, None]).reshape(row_count)
    masked = pixel_modes * live_rows[:, None].astype(jnp.bfloat16)
    own_bins = lax.dynamic_slice_in_dim(mode_bins, own_index * col_count, col_count, 0)
    own_table = bin_table(own_bins)
    full_rows = lax.all_gather(masked, "pix", axis=0, tiled=True)
    carried = lax.all_to_all(weighted_modes, "pix", split_axis=1, concat_axis=0, tiled=True)
    binned = []
    current = carried
    for turn_index in range(ROUNDS):
        current = from_behind(current, "modes", 1)
        owner_index = jnp.mod(own_index - turn_index - 1, cycle_size)
        partner_bins = lax.dynamic_slice_in_dim(
            mode_bins, owner_index * col_count + pix_index * quarter, quarter, 0
        )
        flipped = lax.dot_general(
            current, full_rows, (((0,), (0,)), ((), ())), preferred_element_type=jnp.float32
        )
        binned.append(bin_tile(flipped, partner_bins, own_table))
    summed = lax.psum(jnp.stack(binned), "pix")
    return summed[None]


def solution(mesh):
    in_specs = (P("pix", "modes"), P("pix", "modes"), P(), P("pix", None))
    out_specs = P("modes", None, None, None)
    return jax.shard_map(shards, mesh=mesh, in_specs=in_specs, out_specs=out_specs, check_vma=False)
```

profile of v0, /device:TPU:24, one launch (start us, length us, event | category | flops | bytes accessed | tf_op | source)
XLA Modules:
  0.0 413.8 jit_solution(1360815366173107364)
XLA Ops:
  6.5 0.0 all-gather.2.cloned.1.call-start
  6.5 0.8 compare_convert_fusion
  7.3 0.0 copy-start
  7.3 2.8 broadcast_multiply_fusion
  10.1 0.0 all-gather.2.cloned.1.call-update
  10.2 0.0 all-reduce.2.cloned.1.call-start
  10.2 0.0 copy-done
  10.2 0.7 copy.5
  10.9 77.3 %all_to_all.19 = bf16[512,4,384]{0,2,1:T(8,128)(2,1)S(1)} all-to-all(bf16[512,4,384]{0,2,1:T(8,128)(2,1)S(1)} %bitcast.46), channel_id=1, replica_groups=mesh['modes'=64,'pix'=4] {'pix'}, dimensions={1} | all-to-all | bytes 3145728 | tf_op jit(solution)/shard_map/all_to_all | solution.py:45
  88.2 0.9 copy.6
  89.1 0.1 collective-permute-start
  89.2 19.9 %collective-permute-done = bf16[2048,384]{1,0:T(8,128)(2,1)} collective-permute-done((bf16[2048,384]{1,0:T(8,128)(2,1)S(1)}, bf16[2048,384]{1,0:T(8,128)(2,1)}, u32[]{:S(2)}, u32[]{:S(2)}) %collective-permute-start) | collective-permute-done | bytes 1572896 | tf_op jit(solution)/shard_map/ppermute | solution.py:14
  109.1 0.0 collective-permute-start.1
  109.1 20.0 %collective-permute-done.1 = bf16[2048,384]{1,0:T(8,128)(2,1)S(1)} collective-permute-done((bf16[2048,384]{1,0:T(8,128)(2,1)}, bf16[2048,384]{1,0:T(8,128)(2,1)S(1)}, u32[]{:S(2)}, u32[]{:S(2)}) %collective-permute-start.1) | collective-permute-done | bytes 1572896 | tf_op jit(solution)/shard_map/ppermute | solution.py:14
  129.1 0.9 collective-permute-start.2
  130.0 19.0 %collective-permute-done.2 = bf16[2048,384]{1,0:T(8,128)(2,1)} collective-permute-done((bf16[2048,384]{1,0:T(8,128)(2,1)S(1)}, bf16[2048,384]{1,0:T(8,128)(2,1)}, u32[]{:S(2)}, u32[]{:S(2)}) %collective-permute-start.2) | collective-permute-done | bytes 1572896 | tf_op jit(solution)/shard_map/ppermute | solution.py:14
  149.1 2.8 collective-permute-start.3
  151.9 0.8 dynamic_slice.18
  152.7 0.9 fusion.40
  153.5 15.6 %collective-permute-done.3 = bf16[2048,384]{1,0:T(8,128)(2,1)S(1)} collective-permute-done((bf16[2048,384]{1,0:T(8,128)(2,1)}, bf16[2048,384]{1,0:T(8,128)(2,1)S(1)}, u32[]{:S(2)}, u32[]{:S(2)}) %collective-permute-start.3) | collective-permute-done | bytes 1572896 | tf_op jit(solution)/shard_map/ppermute | solution.py:14
  169.1 5.1 %collective-permute-start.4 = (bf16[2048,384]{1,0:T(8,128)(2,1)S(1)}, bf16[2048,384]{1,0:T(8,128)(2,1)}, u32[]{:S(2)}, u32[]{:S(2)}) collective-permute-start(bf16[2048,384]{1,0:T(8,128)(2,1)S(1)} %collective-permute-done.3), channel_id=1, source_target_pairs={{252,0},{0,4},{4,8},{8,12},{12,16},{16,20},{20,24},{24,28},{28,32}... | collective-permute-start | bytes 4718600 | tf_op jit(solution)/shard_map/ppermute | solution.py:14
  174.3 0.0 all-gather.2.cloned.1.call-done
  174.3 0.0 copy-start.2
  174.3 6.3 %convolution_multiply_fusion.4 = f32[1536,384]{1,0:T(8,128)S(1)} fusion(bf16[2048,1536]{1,0:T(8,128)(2,1)} %all-gather.2.cloned.1.call-done, bf16[2048,384]{1,0:T(8,128)(2,1)} %collective-permute-done), kind=kOutput, calls=%fused_computation.4 | convolution fusion | flops 2416508928 | bytes 10223616 | tf_op jit(solution)/shard_map/dot_general | solution.py:54
  180.6 1.5 fusion.33
  182.1 0.9 fusion.9
  183.0 0.0 copy-done.2
  183.0 3.5 convolution_multiply_fusion.3
  186.5 1.5 fusion.31
  188.0 4.9 %convolution_multiply_fusion.2 = f32[1536,384]{1,0:T(8,128)S(1)} fusion(bf16[2048,1536]{1,0:T(8,128)(2,1)S(1)} %copy-done.2, bf16[2048,384]{1,0:T(8,128)(2,1)} %collective-permute-done.2), kind=kOutput, calls=%fused_computation.2 | convolution fusion | flops 2416508928 | bytes 10223616 | tf_op jit(solution)/shard_map/dot_general | solution.py:54
  192.9 1.5 fusion.29
  194.4 0.9 fusion.7
  195.3 0.9 fusion.5
  196.2 3.7 convolution_multiply_fusion.1
  199.9 1.5 fusion.27
  201.4 0.9 fusion.3
  202.3 0.0 collective-permute-done.4
  202.3 4.9 %convolution_multiply_fusion = f32[1536,384]{1,0:T(8,128)S(1)} fusion(bf16[2048,1536]{1,0:T(8,128)(2,1)S(1)} %copy-done.2, bf16[2048,384]{1,0:T(8,128)(2,1)} %collective-permute-done.4), kind=kOutput, calls=%fused_computation | convolution fusion | flops 2416508928 | bytes 10223616 | tf_op jit(solution)/shard_map/dot_general | solution.py:54
  207.2 1.5 fusion.25
  208.7 0.9 fusion.1
  209.6 0.0 copy-start.1
  209.6 0.7 copy-done.1
  210.3 0.0 all-reduce.2.cloned.1.call-update
  210.4 194.8 %all-reduce.2.cloned.1.call-done = f32[1,5,128,128]{3,2,1,0:T(8,128)} async-done(((f32[1,5,128,128]{3,2,1,0:T(8,128)}), f32[1,5,128,128]{3,2,1,0:T(8,128)}) %all-reduce.2.cloned.1.call-update) | async-done | bytes 327696 | tf_op jit(solution)/shard_map/psum | solution.py:58
  405.2 1.7 copy.12
Async XLA Ops:
  6.5 167.7 %all-gather.2.cloned.1.call-start = ((), (), s32[]{:S(2)}) async-start(), calls=%async_computation.1 | async-start | bytes 7864320 | tf_op jit(solution)/shard_map/all_gather | solution.py:44
  7.3 2.9 copy-start
  10.2 395.0 %all-reduce.2.cloned.1.call-start = ((), (), s32[]{:S(2)}) async-start(), calls=%async_computation.2 | async-start | bytes 655360 | tf_op jit(solution)/shard_map/psum | solution.py:58
  89.1 20.0 %collective-permute-start = (bf16[2048,384]{1,0:T(8,128)(2,1)S(1)}, bf16[2048,384]{1,0:T(8,128)(2,1)}, u32[]{:S(2)}, u32[]{:S(2)}) collective-permute-start(bf16[2048,384]{1,0:T(8,128)(2,1)S(1)} %bitcast.47), channel_id=1, source_target_pairs={{252,0},{0,4},{4,8},{8,12},{12,16},{16,20},{20,24},{24,28},{28,32}... | collective-permute-start | bytes 4718600 | tf_op jit(solution)/shard_map/ppermute | solution.py:14
  109.1 20.1 %collective-permute-start.1 = (bf16[2048,384]{1,0:T(8,128)(2,1)}, bf16[2048,384]{1,0:T(8,128)(2,1)S(1)}, u32[]{:S(2)}, u32[]{:S(2)}) collective-permute-start(bf16[2048,384]{1,0:T(8,128)(2,1)} %collective-permute-done), channel_id=1, source_target_pairs={{252,0},{0,4},{4,8},{8,12},{12,16},{16,20},{20,24},{24,28},{28,32}... | collective-permute-start | bytes 4718600 | tf_op jit(solution)/shard_map/ppermute | solution.py:14
  129.1 19.9 %collective-permute-start.2 = (bf16[2048,384]{1,0:T(8,128)(2,1)S(1)}, bf16[2048,384]{1,0:T(8,128)(2,1)}, u32[]{:S(2)}, u32[]{:S(2)}) collective-permute-start(bf16[2048,384]{1,0:T(8,128)(2,1)S(1)} %collective-permute-done.1), channel_id=1, source_target_pairs={{252,0},{0,4},{4,8},{8,12},{12,16},{16,20},{20,24},{24,28},{28,32}... | collective-permute-start | bytes 4718600 | tf_op jit(solution)/shard_map/ppermute | solution.py:14
  149.1 20.1 %collective-permute-start.3 = (bf16[2048,384]{1,0:T(8,128)(2,1)}, bf16[2048,384]{1,0:T(8,128)(2,1)S(1)}, u32[]{:S(2)}, u32[]{:S(2)}) collective-permute-start(bf16[2048,384]{1,0:T(8,128)(2,1)} %collective-permute-done.2), channel_id=1, source_target_pairs={{252,0},{0,4},{4,8},{8,12},{12,16},{16,20},{20,24},{24,28},{28,32}... | collective-permute-start | bytes 4718600 | tf_op jit(solution)/shard_map/ppermute | solution.py:14
  169.1 33.2 %collective-permute-start.4 = (bf16[2048,384]{1,0:T(8,128)(2,1)S(1)}, bf16[2048,384]{1,0:T(8,128)(2,1)}, u32[]{:S(2)}, u32[]{:S(2)}) collective-permute-start(bf16[2048,384]{1,0:T(8,128)(2,1)S(1)} %collective-permute-done.3), channel_id=1, source_target_pairs={{252,0},{0,4},{4,8},{8,12},{12,16},{16,20},{20,24},{24,28},{28,32}... | collective-permute-start | bytes 4718600 | tf_op jit(solution)/shard_map/ppermute | solution.py:14
  174.3 8.8 %copy-start.2 = (bf16[2048,1536]{1,0:T(8,128)(2,1)S(1)}, bf16[2048,1536]{1,0:T(8,128)(2,1)}, u32[]{:S(2)}) copy-start(bf16[2048,1536]{1,0:T(8,128)(2,1)} %all-gather.2.cloned.1.call-done) | copy-start | bytes 18874372
  209.6 0.7 copy-start.1
Sparse Core Ops, SparseCore 0:
  10.3 135.3 all-gather.1
  210.5 194.6 all-reduce.1
where the time goes:
time: 414 us
  waiting for transfers between devices  270 us (65%)
  blocking collectives  77.3 us (19%)
  matrix products  35.2 us (9%)
  between operations  13.5 us (3%)
  starting transfers between devices  8.95 us (2%)
  local copies, waits for them, and re-layouts  5.65 us (1%)
    psum x1, waiting for transfers between devices, shards(): summed = lax.psum(jnp.stack(binned), 'pix')  195 us
    all_to_all x1, blocking collectives, shards(): lax.all_to_all(weighted_modes, 'pix', split_axis=1, concat_axis=0, tiled=...  77.3 us
    ppermute x5, waiting for transfers between devices, from_behind(): return lax.ppermute(block, axis, route)  74.6 us
    dot_general x5, matrix products, shards(): lax.dot_general(current, full_rows, (((0,), (0,)), ((), ())), preferred_e...  23.3 us
    ppermute x5, starting transfers between devices, from_behind(): return lax.ppermute(block, axis, route)  8.91 us
  transfers between devices with their start and end apart: 7, of which 5 were waited for; matrix products, arithmetic and copies ran while one was open for 8% of the time, Pallas kernels for 0%

commit v1 on v0

v1 whole, which is shorter than its diff:
```python
import jax
import jax.numpy as jnp
from jax import lax
from jax.sharding import PartitionSpec as P

NB = 128
ROW_BLOCK = 128
ROUNDS = 5
CHUNKS = 3
GROUPS = 4
HALF = 32


def move(block, route):
    pairs = []
    for half in range(2):
        for place in range(HALF):
            for p in range(GROUPS):
                target = route(half, place, p)
                if target is not None:
                    source = (half * HALF + place) * GROUPS + p
                    pairs.append((source, (target[0] * HALF + target[1]) * GROUPS + target[2]))
    return lax.ppermute(block, ("modes", "pix"), pairs)


def ahead(distance, core=None, wrap=False):
    def route(half, place, p):
        if core is not None and place % 2 != core:
            return None
        if (place + distance >= HALF) != wrap:
            return None
        return half, (place + distance) % HALF, p

    return route


def across(half, place, p):
    if place < HALF - ROUNDS:
        return None
    return 1 - half, place, GROUPS - 1 - p


def other_core(half, place, p):
    return half, place ^ 1, p


def core_up(half, place, p):
    return (half, place + 1, p) if place % 2 == 0 else None


def pix_partner(k):
    return lambda half, place, p: (half, place, p ^ k)


def bin_table(bin_ids):
    return (bin_ids[:, None] == jnp.arange(NB, dtype=jnp.int32)[None, :]).astype(jnp.float32)


def bin_tile(flipped, partner_bins, own_table):
    squares = flipped * flipped
    partner_table = bin_table(partner_bins)
    left = lax.dot_general(
        partner_table, squares, (((0,), (0,)), ((), ())), precision=lax.Precision.HIGHEST
    )
    return 0.5 * jnp.dot(left, own_table, precision=lax.Precision.HIGHEST).T


def sum_over_pix(part, pix_index):
    rows = NB // GROUPS

    def piece(k):
        return lax.dynamic_slice_in_dim(part, (pix_index ^ k) * rows, rows, 1)

    total = piece(0)
    for k in range(1, GROUPS):
        total = total + move(piece(k), pix_partner(k))
    out = jnp.zeros_like(part)
    for k in range(GROUPS):
        got = total if k == 0 else move(total, pix_partner(k))
        out = lax.dynamic_update_slice_in_dim(out, got, (pix_index ^ k) * rows, 1)
    return out


def shards(pixel_modes, weighted_modes, mode_bins, live_counts):
    row_count, col_count = pixel_modes.shape
    cycle_size = lax.axis_size("modes")
    quarter = col_count // GROUPS
    own_index = lax.axis_index("modes")
    pix_index = lax.axis_index("pix")
    core = own_index % 2
    place = own_index % HALF
    offsets = lax.broadcasted_iota(
        jnp.int32, (live_counts.shape[0], live_counts.shape[1], ROW_BLOCK), 2
    )
    live_rows = (offsets < live_counts[:, :, None]).reshape(row_count)

    carried = lax.all_to_all(weighted_modes, "pix", split_axis=1, concat_axis=0, tiled=True)
    shadow = move(carried, across)
    near = move(carried, ahead(2))
    far = move(carried, ahead(4))
    last = move(carried, ahead(5, core=1))

    masked = pixel_modes * live_rows[:, None].astype(jnp.bfloat16)
    width = col_count // CHUNKS
    full = []
    gate = carried
    for c in range(CHUNKS):
        chunk = masked[:, c * width : (c + 1) * width]
        chunk, _ = lax.optimization_barrier((chunk, gate))
        full.append(lax.all_gather(chunk, "pix", axis=0, tiled=True))
        gate = full[-1]

    near = jnp.where(place < 2, move(shadow, ahead(2, wrap=True)), near)
    far = jnp.where(place < 4, move(shadow, ahead(4, wrap=True)), far)
    last = jnp.where(place < 5, move(shadow, ahead(5, core=1, wrap=True)), last)
    first = move(jnp.where(core == 0, carried, near), other_core)
    third = move(jnp.where(core == 0, near, far), other_core)
    fifth = jnp.where(core == 0, last, move(far, core_up))
    partners = [first, near, third, far, fifth]

    own_bins = lax.dynamic_slice_in_dim(mode_bins, own_index * col_count, col_count, 0)
    own_table = bin_table(own_bins)
    binned = []
    for turn_index in range(ROUNDS):
        owner_index = jnp.mod(own_index - turn_index - 1, cycle_size)
        same_half = owner_index // HALF == own_index // HALF
        which = jnp.where(same_half, pix_index, GROUPS - 1 - pix_index)
        partner_bins = lax.dynamic_slice_in_dim(
            mode_bins, owner_index * col_count + which * quarter, quarter, 0
        )
        total = 0.0
        for c in range(CHUNKS):
            flipped = lax.dot_general(
                partners[turn_index], full[c], (((0,), (0,)), ((), ())),
                preferred_element_type=jnp.float32,
            )
            total = total + bin_tile(flipped, partner_bins, own_table[c * width : (c + 1) * width])
        binned.append(total)
    return sum_over_pix(jnp.stack(binned), pix_index)[None]


def solution(mesh):
    in_specs = (P("pix", "modes"), P("pix", "modes"), P(), P("pix", None))
    out_specs = P("modes", None, None, None)
    return jax.shard_map(shards, mesh=mesh, in_specs=in_specs, out_specs=out_specs, check_vma=False)
```

time: 414 us -> 391 us (0.944)
  blocking collectives: 77.3 us -> 0 us
  starting transfers between devices: 8.95 us -> 34.1 us
  waiting for transfers between devices: 270 us -> 286 us
  other arithmetic: 3.6 us -> 8.04 us
  matrix products: 35.2 us -> 39.5 us
    psum x1 -> x0, waiting for transfers between devices: 195 us -> none  [shards(): summed = lax.psum(jnp.stack(binned), 'pix')]
    all_gather x1 -> x3, waiting for transfers between devices: 0.01 us -> 140 us  [shards(): full.append(lax.all_gather(chunk, 'pix', axis=0, tiled=True))]
    all_to_all x1 -> x0, blocking collectives: 77.3 us -> none  [shards(): lax.all_to_all(weighted_modes, 'pix', split_axis=1, concat_axis=0, tiled=...]
    all_to_all x0 -> x1, waiting for transfers between devices: none -> 36.9 us  [shards(): lax.all_to_all(weighted_modes, 'pix', split_axis=1, concat_axis=0, tiled=...]
    ppermute x5 -> x16, waiting for transfers between devices: 74.6 us -> 110 us  [move(): return lax.ppermute(block, ('modes', 'pix'), pairs)]
    ppermute x5 -> x16, starting transfers between devices: 8.91 us -> 28 us  [move(): return lax.ppermute(block, ('modes', 'pix'), pairs)]
    select_n x0 -> x3, other arithmetic: none -> 6.09 us  [the longest x1 4.08 us: shards(): third = move(jnp.where(core == 0, near, far), other_core)]
    all_to_all x0 -> x1, starting transfers between devices: none -> 6.03 us  [shards(): lax.all_to_all(weighted_modes, 'pix', split_axis=1, concat_axis=0, tiled=...]
  transfers between devices with their start and end apart: 7 -> 20, of which waited for: 5 -> 9; matrix products, arithmetic and copies ran while one was open for 8% -> 10% of each run, Pallas kernels for 0% -> 0%
where the time goes in v1:
time: 391 us; the launch traced here: 390 us
  waiting for transfers between devices  286 us (73%)
  matrix products  39.5 us (10%)
  starting transfers between devices  34.1 us (9%)
  between operations  13.7 us (4%)
  local copies, waits for them, and re-layouts  8.38 us (2%)
  other arithmetic  8.04 us (2%)
    all_gather x3, waiting for transfers between devices, shards(): full.append(lax.all_gather(chunk, 'pix', axis=0, tiled=True))  140 us
    ppermute x16, waiting for transfers between devices, move(): return lax.ppermute(block, ('modes', 'pix'), pairs)  110 us
    all_to_all x1, waiting for transfers between devices, shards(): lax.all_to_all(weighted_modes, 'pix', split_axis=1, concat_axis=0, tiled=...  36.9 us
    ppermute x16, starting transfers between devices, move(): return lax.ppermute(block, ('modes', 'pix'), pairs)  28 us
    dot_general x15, matrix products, shards(): lax.dot_general(partners[turn_index], full[c], (((0,), (0,)), ((), ())),...  23.7 us
    dot_general x15, matrix products, bin_tile(): return 0.5 * jnp.dot(left, own_table, precision=lax.Precision.HIGHEST).T  8.06 us
  transfers between devices with their start and end apart: 20, of which 9 were waited for; matrix products, arithmetic and copies ran while one was open for 10% of the time, Pallas kernels for 0%

profile of v1, /device:TPU:24, one launch (start us, length us, event | category | flops | bytes accessed | tf_op | source)
XLA Modules:
  0.0 390.2 jit_solution(10967946740366986056)
XLA Ops:
  6.5 2.6 copy.5
  9.1 6.0 %all-to-all-start = ((bf16[512,4,384]{0,2,1:T(8,128)(2,1)}), bf16[512,4,384]{0,2,1:T(8,128)(2,1)S(1)}, u32[]{:S(2)}, u32[]{:S(2)}) async-start(bf16[512,4,384]{0,2,1:T(8,128)(2,1)} %bitcast), calls=%async_computation | async-start | bytes 3145728 | tf_op jit(solution)/shard_map/all_to_all | solution.py:97
  15.2 36.9 %all-to-all-done = bf16[512,4,384]{0,2,1:T(8,128)(2,1)S(1)} async-done(((bf16[512,4,384]{0,2,1:T(8,128)(2,1)}), bf16[512,4,384]{0,2,1:T(8,128)(2,1)S(1)}, u32[]{:S(2)}, u32[]{:S(2)}) %all-to-all-start) | async-done | bytes 1572896 | tf_op jit(solution)/shard_map/all_to_all | solution.py:97
  52.1 0.9 copy.6
  53.0 1.8 collective-permute-start
  54.8 1.6 broadcast_multiply_fusion
  56.4 1.2 fusion.80
  57.7 3.1 collective-permute-start.2
  60.8 4.5 %collective-permute-start.5 = (bf16[2048,384]{1,0:T(8,128)(2,1)S(1)}, bf16[2048,384]{1,0:T(8,128)(2,1)}, u32[]{:S(2)}, u32[]{:S(2)}) collective-permute-start(bf16[2048,384]{1,0:T(8,128)(2,1)S(1)} %bitcast.95), channel_id=1, source_target_pairs={{0,16},{1,17},{2,18},{3,19},{4,20},{5,21},{6,22},{7,23},{8,24},{9,... | collective-permute-start | bytes 4718600 | tf_op jit(solution)/shard_map/ppermute | solution.py:23
  65.3 1.8 collective-permute-start.1
  67.1 1.8 collective-permute-start.4
  68.9 0.8 dynamic_slice.30
  69.7 0.9 fusion.81
  70.8 1.3 collective-permute-start.8
  72.1 56.8 %collective-permute-done.2 = bf16[2048,384]{1,0:T(8,128)(2,1)S(1)} collective-permute-done((bf16[2048,384]{1,0:T(8,128)(2,1)S(1)}, bf16[2048,384]{1,0:T(8,128)(2,1)S(1)}, u32[]{:S(2)}, u32[]{:S(2)}) %collective-permute-start.2) | collective-permute-done | bytes 1572896 | tf_op jit(solution)/shard_map/ppermute | solution.py:23
  129.0 1.8 collective-permute-start.7
  130.8 41.9 %collective-permute-done.5 = bf16[2048,384]{1,0:T(8,128)(2,1)} collective-permute-done((bf16[2048,384]{1,0:T(8,128)(2,1)S(1)}, bf16[2048,384]{1,0:T(8,128)(2,1)}, u32[]{:S(2)}, u32[]{:S(2)}) %collective-permute-start.5) | collective-permute-done | bytes 1572896 | tf_op jit(solution)/shard_map/ppermute | solution.py:23
  172.7 4.1 %broadcast_select_fusion.2 = (bf16[2048,384]{1,0:T(8,128)(2,1)}, bf16[2048,384]{1,0:T(8,128)(2,1)}, bf16[2048,384]{1,0:T(8,128)(2,1)S(1)}) fusion(pred[]{:T(512)S(6)} %eq.63, bf16[2048,384]{1,0:T(8,128)(2,1)} %collective-permute-done.4, bf16[2048,384]{1,0:T(8,128)(2,1)} %collective-permute-done.5, pred[]{:T(512)S(6)} %lt.99, ...), kind=kLoop, calls=%fused_computation.3 | loop fusion | flops 2359296 | bytes 11010051 | tf_op jit(solution)/shard_map/jit(_where)/select_n | solution.py:117
  176.8 2.5 collective-permute-start.9
  179.4 3.2 convolution_multiply_fusion.5
  182.6 0.5 fusion.40
  183.5 1.0 convolution_multiply_fusion.11
  185.4 1.0 fusion.31
  186.7 1.7 select_select_fusion
  188.4 1.0 convolution_multiply_fusion.2
  189.4 0.5 fusion.37
  190.3 1.0 convolution_multiply_fusion.8
  191.9 1.0 fusion.29
  192.9 1.0 convolution_multiply_fusion.14
  194.6 1.0 fusion.33
  195.6 102.0 %all-gather.6.cloned.1.call-done = bf16[2048,512]{1,0:T(8,128)(2,1)} async-done(((bf16[512,512]{1,0:T(8,128)(2,1)}), bf16[2048,512]{1,0:T(8,128)(2,1)}) %all-gather.6.cloned.1.call-update) | async-done | bytes 2097168 | tf_op jit(solution)/shard_map/all_gather | solution.py:110
  297.7 2.7 convolution_multiply_fusion.1
  300.4 0.5 fusion.36
  300.9 2.4 convolution_multiply_fusion.4
  303.7 0.5 fusion.39
  304.8 1.0 convolution_multiply_fusion.7
  305.8 0.5 fusion.42
  306.6 1.0 convolution_multiply_fusion.10
  307.7 0.5 fusion.45
  308.2 1.0 convolution_add_fusion.7
  309.1 1.0 convolution_multiply_fusion.13
  310.1 0.5 fusion.48
  310.7 1.0 convolution_add_fusion.9
  311.6 37.6 %all-gather.8.cloned.1.call-done = bf16[2048,512]{1,0:T(8,128)(2,1)} async-done(((bf16[512,512]{1,0:T(8,128)(2,1)}), bf16[2048,512]{1,0:T(8,128)(2,1)}) %all-gather.8.cloned.1.call-update) | async-done | bytes 2097168 | tf_op jit(solution)/shard_map/all_gather | solution.py:110
  349.3 2.7 convolution_multiply_fusion
  352.0 0.7 fusion.35
  352.8 2.5 convolution_multiply_fusion.3
  355.8 1.0 convolution_multiply_fusion.6
  357.4 1.0 convolution_multiply_fusion.9
  358.4 0.5 fusion.44
  358.9 1.0 convolution_multiply_fusion.12
  359.9 0.5 fusion.47
  362.2 0.7 collective-permute-start.10
  362.8 1.4 collective-permute-start.11
  364.2 2.4 collective-permute-start.12
  366.6 0.6 collective-permute-done.10
  367.2 4.9 %collective-permute-done.11 = f32[5,32,128]{2,1,0:T(8,128)S(1)} collective-permute-done((f32[5,32,128]{2,1,0:T(8,128)S(1)}, f32[5,32,128]{2,1,0:T(8,128)S(1)}, u32[]{:S(2)}, u32[]{:S(2)}) %collective-permute-start.11) | collective-permute-done | bytes 81952 | tf_op jit(solution)/shard_map/ppermute | solution.py:23
  372.2 1.5 collective-permute-start.13
  373.7 1.4 collective-permute-start.14
  375.2 1.5 collective-permute-start.15
  376.7 0.9 collective-permute-done.13
  377.5 4.8 %collective-permute-done.14 = f32[5,32,128]{2,1,0:T(8,128)S(1)} collective-permute-done((f32[5,32,128]{2,1,0:T(8,128)S(1)}, f32[5,32,128]{2,1,0:T(8,128)S(1)}, u32[]{:S(2)}, u32[]{:S(2)}) %collective-permute-start.14) | collective-permute-done | bytes 81952 | tf_op jit(solution)/shard_map/ppermute | solution.py:23
  382.4 0.7 copy-done.1
  383.1 0.6 bitcast_dynamic-update-slice_fusion
  (79 shorter events, 7.8 us)
Async XLA Ops:
  9.1 6.0 %copy-start.9 = (s32[2,2]{1,0:T(2,128)S(1)}, s32[2,2]{1,0:T(2,128)}, u32[]{:S(2)}) copy-start(s32[2,2]{1,0:T(2,128)} %param.7) | copy-start | bytes 52
  9.1 43.0 %all-to-all-start = ((bf16[512,4,384]{0,2,1:T(8,128)(2,1)}), bf16[512,4,384]{0,2,1:T(8,128)(2,1)S(1)}, u32[]{:S(2)}, u32[]{:S(2)}) async-start(bf16[512,4,384]{0,2,1:T(8,128)(2,1)} %bitcast), calls=%async_computation | async-start | bytes 3145728 | tf_op jit(solution)/shard_map/all_to_all | solution.py:97
  15.2 164.1 %all-gather.4.cloned.1.call-start = ((), (), s32[]{:S(2)}) async-start(), calls=%async_computation.1 | async-start | bytes 2621440 | tf_op jit(solution)/shard_map/all_gather | solution.py:110
  53.0 12.3 %collective-permute-start = (bf16[2048,384]{1,0:T(8,128)(2,1)S(1)}, bf16[2048,384]{1,0:T(8,128)(2,1)}, u32[]{:S(2)}, u32[]{:S(2)}) collective-permute-start(bf16[2048,384]{1,0:T(8,128)(2,1)S(1)} %bitcast.93), channel_id=1, source_target_pairs={{108,239},{109,238},{110,237},{111,236},{112,243},{113,242},{114,2... | collective-permute-start | bytes 4718600 | tf_op jit(solution)/shard_map/ppermute | solution.py:23
  57.6 240.0 %all-gather.6.cloned.1.call-start = ((), (), s32[]{:S(2)}) async-start(), calls=%async_computation.2 | async-start | bytes 2621440 | tf_op jit(solution)/shard_map/all_gather | solution.py:110
  57.7 71.3 %collective-permute-start.2 = (bf16[2048,384]{1,0:T(8,128)(2,1)S(1)}, bf16[2048,384]{1,0:T(8,128)(2,1)S(1)}, u32[]{:S(2)}, u32[]{:S(2)}) collective-permute-start(bf16[2048,384]{1,0:T(8,128)(2,1)S(1)} %bitcast.94), channel_id=1, source_target_pairs={{0,8},{1,9},{2,10},{3,11},{4,12},{5,13},{6,14},{7,15},{8,16},{9,17... | collective-permute-start | bytes 4718600 | tf_op jit(solution)/shard_map/ppermute | solution.py:23
  60.8 111.9 %collective-permute-start.5 = (bf16[2048,384]{1,0:T(8,128)(2,1)S(1)}, bf16[2048,384]{1,0:T(8,128)(2,1)}, u32[]{:S(2)}, u32[]{:S(2)}) collective-permute-start(bf16[2048,384]{1,0:T(8,128)(2,1)S(1)} %bitcast.95), channel_id=1, source_target_pairs={{0,16},{1,17},{2,18},{3,19},{4,20},{5,21},{6,22},{7,23},{8,24},{9,... | collective-permute-start | bytes 4718600 | tf_op jit(solution)/shard_map/ppermute | solution.py:23
  65.3 107.4 %collective-permute-start.1 = (bf16[2048,384]{1,0:T(8,128)(2,1)}, bf16[2048,384]{1,0:T(8,128)(2,1)}, u32[]{:S(2)}, u32[]{:S(2)}) collective-permute-start(bf16[2048,384]{1,0:T(8,128)(2,1)} %collective-permute-done), channel_id=1, source_target_pairs={{120,0},{121,1},{122,2},{123,3},{124,4},{125,5},{126,6},{127,7},{2... | collective-permute-start | bytes 4718600 | tf_op jit(solution)/shard_map/ppermute | solution.py:23
  67.1 105.6 %collective-permute-start.4 = (bf16[2048,384]{1,0:T(8,128)(2,1)}, bf16[2048,384]{1,0:T(8,128)(2,1)}, u32[]{:S(2)}, u32[]{:S(2)}) collective-permute-start(bf16[2048,384]{1,0:T(8,128)(2,1)} %collective-permute-done), channel_id=1, source_target_pairs={{112,0},{113,1},{114,2},{115,3},{116,4},{117,5},{118,6},{119,7},{1... | collective-permute-start | bytes 4718600 | tf_op jit(solution)/shard_map/ppermute | solution.py:23
  70.6 229.8 %copy-start.7 = (s32[384]{0:T(512)}, s32[384]{0:T(512)S(1)}, u32[]{:S(2)}) copy-start(s32[384]{0:T(512)S(1)} %get-tuple-element.19) | copy-start | bytes 4612
  70.8 115.9 %collective-permute-start.8 = (bf16[2048,384]{1,0:T(8,128)(2,1)S(1)}, bf16[2048,384]{1,0:T(8,128)(2,1)}, u32[]{:S(2)}, u32[]{:S(2)}) collective-permute-start(bf16[2048,384]{1,0:T(8,128)(2,1)S(1)} %bitcast.96), channel_id=1, source_target_pairs={{4,24},{5,25},{6,26},{7,27},{12,32},{13,33},{14,34},{15,35},{20,40... | collective-permute-start | bytes 4718600 | tf_op jit(solution)/shard_map/ppermute | solution.py:23
  129.0 43.7 %copy-start = (bf16[2048,384]{1,0:T(8,128)(2,1)}, bf16[2048,384]{1,0:T(8,128)(2,1)S(1)}, u32[]{:S(2)}) copy-start(bf16[2048,384]{1,0:T(8,128)(2,1)S(1)} %collective-permute-done.2) | copy-start | bytes 4718596
  129.0 57.7 %collective-permute-start.7 = (bf16[2048,384]{1,0:T(8,128)(2,1)}, bf16[2048,384]{1,0:T(8,128)(2,1)}, u32[]{:S(2)}, u32[]{:S(2)}) collective-permute-start(bf16[2048,384]{1,0:T(8,128)(2,1)} %collective-permute-done), channel_id=1, source_target_pairs={{108,0},{109,1},{110,2},{111,3},{116,8},{117,9},{118,10},{119,11},... | collective-permute-start | bytes 4718600 | tf_op jit(solution)/shard_map/ppermute | solution.py:23
  176.8 9.9 %collective-permute-start.9 = (bf16[2048,384]{1,0:T(8,128)(2,1)}, bf16[2048,384]{1,0:T(8,128)(2,1)}, u32[]{:S(2)}, u32[]{:S(2)}) collective-permute-start(bf16[2048,384]{1,0:T(8,128)(2,1)} %get-tuple-element.14), channel_id=1, source_target_pairs={{0,4},{1,5},{2,6},{3,7},{8,12},{9,13},{10,14},{11,15},{16,20},{17,... | collective-permute-start | bytes 4718600 | tf_op jit(solution)/shard_map/ppermute | solution.py:23
  179.3 170.0 %all-gather.8.cloned.1.call-start = ((), (), s32[]{:S(2)}) async-start(), calls=%async_computation.3 | async-start | bytes 2621440 | tf_op jit(solution)/shard_map/all_gather | solution.py:110
  179.3 4.2 %copy-start.10 = (bf16[2048,512]{1,0:T(8,128)(2,1)S(1)}, bf16[2048,512]{1,0:T(8,128)(2,1)}, u32[]{:S(2)}) copy-start(bf16[2048,512]{1,0:T(8,128)(2,1)} %all-gather.4.cloned.1.call-done) | copy-start | bytes 6291460
  179.3 10.9 %collective-permute-start.6 = (bf16[2048,384]{1,0:T(8,128)(2,1)}, bf16[2048,384]{1,0:T(8,128)(2,1)S(1)}, u32[]{:S(2)}, u32[]{:S(2)}) collective-permute-start(bf16[2048,384]{1,0:T(8,128)(2,1)} %get-tuple-element.13), channel_id=1, source_target_pairs={{0,4},{1,5},{2,6},{3,7},{4,0},{5,1},{6,2},{7,3},{8,12},{9,13},{10,... | collective-permute-start | bytes 4718600 | tf_op jit(solution)/shard_map/ppermute | solution.py:23
  186.3 6.6 %collective-permute-start.3 = (bf16[2048,384]{1,0:T(8,128)(2,1)S(1)}, bf16[2048,384]{1,0:T(8,128)(2,1)S(1)}, u32[]{:S(2)}, u32[]{:S(2)}) collective-permute-start(bf16[2048,384]{1,0:T(8,128)(2,1)S(1)} %broadcast_select_fusion.3), channel_id=1, source_target_pairs={{0,4},{1,5},{2,6},{3,7},{4,0},{5,1},{6,2},{7,3},{8,12},{9,13},{10,... | collective-permute-start | bytes 4718600 | tf_op jit(solution)/shard_map/ppermute | solution.py:23
  190.3 1.2 copy-start.13
  192.9 1.2 copy-start.16
  297.6 3.3 copy-start.11
  303.4 1.4 copy-start.14
  304.8 1.5 copy-start.6
  306.6 1.5 copy-start.4
  306.6 2.5 copy-start.17
  309.1 1.5 copy-start.5
  349.3 2.8 copy-start.8
  349.3 3.5 copy-start.12
  352.8 3.1 copy-start.15
  357.4 1.5 copy-start.18
  358.9 1.5 copy-start.3
  358.9 1.9 copy-start.2
  362.2 5.0 %collective-permute-start.10 = (f32[5,32,128]{2,1,0:T(8,128)S(1)}, f32[5,32,128]{2,1,0:T(8,128)S(1)}, u32[]{:S(2)}, u32[]{:S(2)}) collective-permute-start(f32[5,32,128]{2,1,0:T(8,128)S(1)} %get-tuple-element.24), channel_id=1, source_target_pairs={{0,1},{1,0},{2,3},{3,2},{4,5},{5,4},{6,7},{7,6},{8,9},{9,8},{10,11... | collective-permute-start | bytes 245768 | tf_op jit(solution)/shard_map/ppermute | solution.py:23
  362.8 9.3 %collective-permute-start.11 = (f32[5,32,128]{2,1,0:T(8,128)S(1)}, f32[5,32,128]{2,1,0:T(8,128)S(1)}, u32[]{:S(2)}, u32[]{:S(2)}) collective-permute-start(f32[5,32,128]{2,1,0:T(8,128)S(1)} %get-tuple-element.26), channel_id=1, source_target_pairs={{0,2},{1,3},{2,0},{3,1},{4,6},{5,7},{6,4},{7,5},{8,10},{9,11},{10,... | collective-permute-start | bytes 245768 | tf_op jit(solution)/shard_map/ppermute | solution.py:23
  364.2 7.9 %collective-permute-start.12 = (f32[5,32,128]{2,1,0:T(8,128)S(1)}, f32[5,32,128]{2,1,0:T(8,128)S(1)}, u32[]{:S(2)}, u32[]{:S(2)}) collective-permute-start(f32[5,32,128]{2,1,0:T(8,128)S(1)} %get-tuple-element.25), channel_id=1, source_target_pairs={{0,3},{1,2},{2,1},{3,0},{4,7},{5,6},{6,5},{7,4},{8,11},{9,10},{10,... | collective-permute-start | bytes 245768 | tf_op jit(solution)/shard_map/ppermute | solution.py:23
  372.2 5.3 %collective-permute-start.13 = (f32[5,32,128]{2,1,0:T(8,128)S(1)}, f32[5,32,128]{2,1,0:T(8,128)S(1)}, u32[]{:S(2)}, u32[]{:S(2)}) collective-permute-start(f32[5,32,128]{2,1,0:T(8,128)S(1)} %get-tuple-element.12), channel_id=1, source_target_pairs={{0,1},{1,0},{2,3},{3,2},{4,5},{5,4},{6,7},{7,6},{8,9},{9,8},{10,11... | collective-permute-start | bytes 245768 | tf_op jit(solution)/shard_map/ppermute | solution.py:23
  373.7 8.6 %collective-permute-start.14 = (f32[5,32,128]{2,1,0:T(8,128)S(1)}, f32[5,32,128]{2,1,0:T(8,128)S(1)}, u32[]{:S(2)}, u32[]{:S(2)}) collective-permute-start(f32[5,32,128]{2,1,0:T(8,128)S(1)} %get-tuple-element.12), channel_id=1, source_target_pairs={{0,2},{1,3},{2,0},{3,1},{4,6},{5,7},{6,4},{7,5},{8,10},{9,11},{10,... | collective-permute-start | bytes 245768 | tf_op jit(solution)/shard_map/ppermute | solution.py:23
  375.2 7.2 %collective-permute-start.15 = (f32[5,32,128]{2,1,0:T(8,128)S(1)}, f32[5,32,128]{2,1,0:T(8,128)S(1)}, u32[]{:S(2)}, u32[]{:S(2)}) collective-permute-start(f32[5,32,128]{2,1,0:T(8,128)S(1)} %get-tuple-element.12), channel_id=1, source_target_pairs={{0,3},{1,2},{2,1},{3,0},{4,7},{5,6},{6,5},{7,4},{8,11},{9,10},{10,... | collective-permute-start | bytes 245768 | tf_op jit(solution)/shard_map/ppermute | solution.py:23
  382.3 0.7 copy-start.1
Sparse Core Ops, SparseCore 0:
  57.8 51.3 all-gather.3
  179.4 118.1 all-gather.5
  299.4 49.7 all-gather.7

commit v2 on v1

--- a/solution.py
+++ b/solution.py
@@ -6,7 +6,6 @@
 NB = 128
 ROW_BLOCK = 128
 ROUNDS = 5
-CHUNKS = 3
 GROUPS = 4
 HALF = 32
 
@@ -23,21 +22,39 @@
     return lax.ppermute(block, ("modes", "pix"), pairs)
 
 
-def ahead(distance, core=None, wrap=False):
+def spot(place):
+    return place // 8, (place // 2) % 4, place % 2
+
+
+def seat(x, y, core):
+    return (x * 4 + y) * 2 + core
+
+
+def trails(y, core):
+    return 2 * y + core >= 8 - ROUNDS
+
+
+def next_row(half, place, p):
+    x, y, core = spot(place)
+    return (half, seat(x + 1, y, core), p) if x < 3 and trails(y, core) else None
+
+
+def next_half(k):
     def route(half, place, p):
-        if core is not None and place % 2 != core:
-            return None
-        if (place + distance >= HALF) != wrap:
-            return None
-        return half, (place + distance) % HALF, p
+        x, y, core = spot(place)
+        return (1 - half, seat(0, y, core), (GROUPS - 1 - p) ^ k) if x == 3 and trails(y, core) else None
 
     return route
 
 
-def across(half, place, p):
-    if place < HALF - ROUNDS:
-        return None
-    return 1 - half, place, GROUPS - 1 - p
+def along_row(chips, wrap, last=False):
+    def route(half, place, p):
+        x, y, core = spot(place)
+        if (y + chips >= 4) != wrap or (last and core == 0):
+            return None
+        return half, seat(x, (y + chips) % 4, 0 if last else core), p
+
+    return route
 
 
 def other_core(half, place, p):
@@ -87,32 +104,30 @@
     quarter = col_count // GROUPS
     own_index = lax.axis_index("modes")
     pix_index = lax.axis_index("pix")
-    core = own_index % 2
-    place = own_index % HALF
+    x, y, core = spot(own_index % HALF)
     offsets = lax.broadcasted_iota(
         jnp.int32, (live_counts.shape[0], live_counts.shape[1], ROW_BLOCK), 2
     )
     live_rows = (offsets < live_counts[:, :, None]).reshape(row_count)
 
+    masked = pixel_modes * live_rows[:, None].astype(jnp.bfloat16)
+    full = lax.all_gather(masked, "pix", axis=0, tiled=True)
     carried = lax.all_to_all(weighted_modes, "pix", split_axis=1, concat_axis=0, tiled=True)
-    shadow = move(carried, across)
-    near = move(carried, ahead(2))
-    far = move(carried, ahead(4))
-    last = move(carried, ahead(5, core=1))
 
-    masked = pixel_modes * live_rows[:, None].astype(jnp.bfloat16)
-    width = col_count // CHUNKS
-    full = []
-    gate = carried
-    for c in range(CHUNKS):
-        chunk = masked[:, c * width : (c + 1) * width]
-        chunk, _ = lax.optimization_barrier((chunk, gate))
-        full.append(lax.all_gather(chunk, "pix", axis=0, tiled=True))
-        gate = full[-1]
+    crossed = jnp.zeros_like(carried)
+    for k in range(GROUPS):
+        target = (GROUPS - 1 - pix_index) ^ k
+        piece = lax.dynamic_slice_in_dim(weighted_modes, target * quarter, quarter, 1)
+        got = move(piece, next_half(k))
+        source = (pix_index ^ k) ^ (GROUPS - 1)
+        crossed = lax.dynamic_update_slice_in_dim(crossed, got, source * row_count, 0)
+    previous = jnp.where(x == 0, crossed, move(carried, next_row))
 
-    near = jnp.where(place < 2, move(shadow, ahead(2, wrap=True)), near)
-    far = jnp.where(place < 4, move(shadow, ahead(4, wrap=True)), far)
-    last = jnp.where(place < 5, move(shadow, ahead(5, core=1, wrap=True)), last)
+    near = jnp.where(y < 1, move(previous, along_row(1, True)), move(carried, along_row(1, False)))
+    far = jnp.where(y < 2, move(previous, along_row(2, True)), move(carried, along_row(2, False)))
+    last = jnp.where(
+        y < 3, move(previous, along_row(3, True, True)), move(carried, along_row(3, False, True))
+    )
     first = move(jnp.where(core == 0, carried, near), other_core)
     third = move(jnp.where(core == 0, near, far), other_core)
     fifth = jnp.where(core == 0, last, move(far, core_up))
@@ -123,18 +138,13 @@
     binned = []
     for turn_index in range(ROUNDS):
         owner_index = jnp.mod(own_index - turn_index - 1, cycle_size)
-        same_half = owner_index // HALF == own_index // HALF
-        which = jnp.where(same_half, pix_index, GROUPS - 1 - pix_index)
         partner_bins = lax.dynamic_slice_in_dim(
-            mode_bins, owner_index * col_count + which * quarter, quarter, 0
+            mode_bins, owner_index * col_count + pix_index * quarter, quarter, 0
         )
-        total = 0.0
-        for c in range(CHUNKS):
-            flipped = lax.dot_general(
-                partners[turn_index], full[c], (((0,), (0,)), ((), ())),
-                preferred_element_type=jnp.float32,
-            )
-            total = total + bin_tile(flipped, partner_bins, own_table[c * width : (c + 1) * width])
+        flipped = lax.dot_general(
+            partners[turn_index], full, (((0,), (0,)), ((), ())), preferred_element_type=jnp.float32
+        )
+        total = bin_tile(flipped, partner_bins, own_table)
         binned.append(total)
     return sum_over_pix(jnp.stack(binned), pix_index)[None]
 

time: 391 us -> 350 us (0.90)
  waiting for transfers between devices: 286 us -> 132 us
  blocking collectives: 0 us -> 82.2 us
  starting transfers between devices: 34.1 us -> 65.6 us
  matrix products: 39.5 us -> 29.4 us
  local copies, waits for them, and re-layouts: 8.38 us -> 12.4 us
    all_gather x3 -> x1, waiting for transfers between devices: 140 us -> 0.01 us  [shards(): full = lax.all_gather(masked, 'pix', axis=0, tiled=True)]
    all_to_all x0 -> x1, blocking collectives: none -> 82.2 us  [shards(): lax.all_to_all(weighted_modes, 'pix', split_axis=1, concat_axis=0, tiled=...]
    ppermute x16 -> x20, starting transfers between devices: 28 us -> 65.6 us  [move(): return lax.ppermute(block, ('modes', 'pix'), pairs)]
    all_to_all x1 -> x0, waiting for transfers between devices: 36.9 us -> none  [shards(): lax.all_to_all(weighted_modes, 'pix', split_axis=1, concat_axis=0, tiled=...]
    ppermute x16 -> x20, waiting for transfers between devices: 110 us -> 132 us  [move(): return lax.ppermute(block, ('modes', 'pix'), pairs)]
    all_to_all x1 -> x0, starting transfers between devices: 6.03 us -> none  [shards(): lax.all_to_all(weighted_modes, 'pix', split_axis=1, concat_axis=0, tiled=...]
    dot_general x15 -> x5, matrix products: 23.7 us -> 19 us  [shards(): lax.dot_general(partners[turn_index], full, (((0,), (0,)), ((), ())), pre...]
    dot_general x15 -> x5, matrix products: 8.06 us -> 4.68 us  [bin_tile(): return 0.5 * jnp.dot(left, own_table, precision=lax.Precision.HIGHEST).T]
  transfers between devices with their start and end apart: 20 -> 21, of which waited for: 9 -> 10; matrix products, arithmetic and copies ran while one was open for 10% -> 11% of each run, Pallas kernels for 0% -> 0%
where the time goes in v2:
time: 350 us; the launch traced here: 346 us
  waiting for transfers between devices  132 us (38%)
  blocking collectives  82.2 us (23%)
  starting transfers between devices  65.6 us (19%)
  matrix products  29.4 us (8%)
  between operations  13.8 us (4%)
  local copies, waits for them, and re-layouts  12.4 us (4%)
  other arithmetic  10 us (3%)
    ppermute x20, waiting for transfers between devices, move(): return lax.ppermute(block, ('modes', 'pix'), pairs)  132 us
    all_to_all x1, blocking collectives, shards(): lax.all_to_all(weighted_modes, 'pix', split_axis=1, concat_axis=0, tiled=...  82.2 us
    ppermute x20, starting transfers between devices, move(): return lax.ppermute(block, ('modes', 'pix'), pairs)  65.6 us
    dot_general x5, matrix products, shards(): lax.dot_general(partners[turn_index], full, (((0,), (0,)), ((), ())), pre...  19 us
  transfers between devices with their start and end apart: 21, of which 10 were waited for; matrix products, arithmetic and copies ran while one was open for 11% of the time, Pallas kernels for 0%

profile of v2, /device:TPU:24, one launch (start us, length us, event | category | flops | bytes accessed | tf_op | source)
XLA Modules:
  0.0 345.6 jit_solution(14434295742788985408)
XLA Ops:
  6.5 0.8 compare_convert_fusion
  7.3 2.8 broadcast_multiply_fusion
  10.1 0.0 all-gather.2.cloned.1.call-update
  10.1 1.4 copy-done.3
  11.5 0.7 copy.6
  12.2 0.9 copy.7
  13.1 82.2 %all_to_all.19 = bf16[512,4,384]{2,0,1:T(8,128)(2,1)S(1)} all-to-all(bf16[512,4,384]{2,0,1:T(8,128)(2,1)S(1)} %copy.7), channel_id=1, replica_groups=mesh['modes'=64,'pix'=4] {'pix'}, dimensions={1} | all-to-all | bytes 3145728 | tf_op jit(solution)/shard_map/all_to_all | solution.py:115
  95.3 3.5 %collective-permute-start.4 = (bf16[2048,384]{1,0:T(8,128)(2,1)S(1)}, bf16[2048,384]{1,0:T(8,128)(2,1)S(1)}, u32[]{:S(2)}, u32[]{:S(2)}) collective-permute-start(bf16[2048,384]{1,0:T(8,128)(2,1)S(1)} %bitcast.53), channel_id=1, source_target_pairs={{12,44},{13,45},{14,46},{15,47},{16,48},{17,49},{18,50},{19,51},{2... | collective-permute-start | bytes 4718600 | tf_op jit(solution)/shard_map/ppermute | solution.py:22
  98.8 2.6 constant_dynamic-slice_fusion.3
  101.4 1.3 collective-permute-start
  102.7 1.3 collective-permute-start.1
  104.0 1.3 collective-permute-start.2
  105.3 1.3 collective-permute-start.3
  106.7 28.8 %collective-permute-done = bf16[512,384]{1,0:T(8,128)(2,1)} collective-permute-done((bf16[512,384]{1,0:T(8,128)(2,1)}, bf16[512,384]{1,0:T(8,128)(2,1)}, u32[]{:S(2)}, u32[]{:S(2)}) %collective-permute-start) | collective-permute-done | bytes 393248 | tf_op jit(solution)/shard_map/ppermute | solution.py:22
  135.5 0.1 broadcast_in_dim.13
  135.6 1.1 constant_dynamic-update-slice_fusion.3
  136.7 36.7 %collective-permute-done.1 = bf16[512,384]{1,0:T(8,128)(2,1)} collective-permute-done((bf16[512,384]{1,0:T(8,128)(2,1)}, bf16[512,384]{1,0:T(8,128)(2,1)}, u32[]{:S(2)}, u32[]{:S(2)}) %collective-permute-start.1) | collective-permute-done | bytes 393248 | tf_op jit(solution)/shard_map/ppermute | solution.py:22
  173.4 1.1 constant_dynamic-update-slice_fusion.2
  174.5 1.1 constant_dynamic-update-slice_fusion.1
  175.5 0.1 constant_dynamic-update-slice_fusion
  175.6 1.3 collective-permute-start.9
  176.9 1.3 collective-permute-start.6
  178.2 1.4 broadcast_select_fusion.1
  179.6 7.9 %collective-permute-start.8 = (bf16[2048,384]{1,0:T(8,128)(2,1)}, bf16[2048,384]{1,0:T(8,128)(2,1)S(1)}, u32[]{:S(2)}, u32[]{:S(2)}) collective-permute-start(bf16[2048,384]{1,0:T(8,128)(2,1)} %broadcast_select_fusion.1), channel_id=1, source_target_pairs={{16,0},{17,1},{18,2},{19,3},{20,4},{21,5},{22,6},{23,7},{24,8},{25... | collective-permute-start | bytes 4718600 | tf_op jit(solution)/shard_map/ppermute | solution.py:22
  187.5 4.1 %collective-permute-start.5 = (bf16[2048,384]{1,0:T(8,128)(2,1)}, bf16[2048,384]{1,0:T(8,128)(2,1)}, u32[]{:S(2)}, u32[]{:S(2)}) collective-permute-start(bf16[2048,384]{1,0:T(8,128)(2,1)} %broadcast_select_fusion.1), channel_id=1, source_target_pairs={{24,0},{25,1},{26,2},{27,3},{28,4},{29,5},{30,6},{31,7},{56,32},{5... | collective-permute-start | bytes 4718600 | tf_op jit(solution)/shard_map/ppermute | solution.py:22
  191.6 15.0 %collective-permute-done.9 = bf16[2048,384]{1,0:T(8,128)(2,1)} collective-permute-done((bf16[2048,384]{1,0:T(8,128)(2,1)S(1)}, bf16[2048,384]{1,0:T(8,128)(2,1)}, u32[]{:S(2)}, u32[]{:S(2)}) %collective-permute-start.9) | collective-permute-done | bytes 1572896 | tf_op jit(solution)/shard_map/ppermute | solution.py:22
  206.6 9.6 %collective-permute-done.6 = bf16[2048,384]{1,0:T(8,128)(2,1)} collective-permute-done((bf16[2048,384]{1,0:T(8,128)(2,1)S(1)}, bf16[2048,384]{1,0:T(8,128)(2,1)}, u32[]{:S(2)}, u32[]{:S(2)}) %collective-permute-start.6) | collective-permute-done | bytes 1572896 | tf_op jit(solution)/shard_map/ppermute | solution.py:22
  216.3 1.1 copy-done.4
  217.4 31.5 %collective-permute-done.5 = bf16[2048,384]{1,0:T(8,128)(2,1)} collective-permute-done((bf16[2048,384]{1,0:T(8,128)(2,1)}, bf16[2048,384]{1,0:T(8,128)(2,1)}, u32[]{:S(2)}, u32[]{:S(2)}) %collective-permute-start.5) | collective-permute-done | bytes 1572896 | tf_op jit(solution)/shard_map/ppermute | solution.py:22
  248.9 3.5 %broadcast_select_fusion.3 = (bf16[2048,384]{1,0:T(8,128)(2,1)}, bf16[2048,384]{1,0:T(8,128)(2,1)S(1)}, bf16[2048,384]{1,0:T(8,128)(2,1)S(1)}) fusion(pred[]{:T(512)S(6)} %eq.101, bf16[2048,384]{1,0:T(8,128)(2,1)} %copy-done.4, bf16[2048,384]{1,0:T(8,128)(2,1)} %collective-permute-done.9, pred[]{:T(512)S(6)} %lt.136, ...), kind=kLoop, calls=%fused_computation.12 | loop fusion | flops 2359296 | bytes 11010051 | tf_op jit(solution)/shard_map/jit(_where)/select_n | solution.py:132
  252.4 1.5 broadcast_select_fusion.4
  253.9 0.8 dynamic_slice.42
  254.7 0.9 fusion.34
  255.6 1.3 collective-permute-start.12
  256.9 1.8 collective-permute-start.11
  258.7 1.7 collective-permute-start.10
  260.3 3.0 collective-permute-start.13
  263.4 5.6 %convolution_multiply_fusion.4 = f32[384,1536]{1,0:T(8,128)S(1)} fusion(bf16[2048,384]{1,0:T(8,128)(2,1)} %collective-permute-done.7, bf16[2048,1536]{1,0:T(8,128)(2,1)} %all-gather.2.cloned.1.call-done), kind=kOutput, calls=%fused_computation.4 | convolution fusion | flops 2416508928 | bytes 10223616 | tf_op jit(solution)/shard_map/dot_general | solution.py:144
  269.0 1.2 fusion.24
  270.1 0.9 fusion.13
  271.1 2.6 convolution_multiply_fusion.3
  273.7 1.2 fusion.25
  274.9 4.0 %convolution_multiply_fusion.2 = f32[384,1536]{1,0:T(8,128)S(1)} fusion(bf16[2048,384]{1,0:T(8,128)(2,1)} %collective-permute-done.10, bf16[2048,1536]{1,0:T(8,128)(2,1)S(1)} %copy-done), kind=kOutput, calls=%fused_computation.2 | convolution fusion | flops 2416508928 | bytes 10223616 | tf_op jit(solution)/shard_map/dot_general | solution.py:144
  278.9 1.2 fusion.26
  280.1 0.9 fusion.11
  281.0 0.9 fusion.9
  281.9 2.6 convolution_multiply_fusion.1
  284.5 1.2 fusion.27
  285.7 1.1 fusion.7
  286.9 4.1 %convolution_multiply_fusion = f32[384,1536]{1,0:T(8,128)S(1)} fusion(bf16[2048,1536]{1,0:T(8,128)(2,1)S(1)} %copy-done, bf16[2048,384]{1,0:T(8,128)(2,1)} %collective-permute-done.13, bf16[2048,384]{1,0:T(8,128)(2,1)} %collective-permute-done.11, bf16[2048,384]{1,0:T(8,128)(2,1)} %collective-permute-done.12, pred[]{:T(512)S(6)} %lt.141, pred[]{:T(512)S(6)} %eq.101), kind=kOutput, calls=%fused_computation | convolution fusion | flops 2418081792 | bytes 13369346 | tf_op jit(solution)/shard_map/dot_general | solution.py:144
  290.9 1.2 fusion.28
  292.1 0.9 fusion.5
  293.0 0.3 collective-permute-start.16
  293.4 29.3 %collective-permute-start.15 = (f32[5,32,128]{2,1,0:T(8,128)S(1)}, f32[5,32,128]{2,1,0:T(8,128)S(1)}, u32[]{:S(2)}, u32[]{:S(2)}) collective-permute-start(f32[5,32,128]{2,1,0:T(8,128)S(1)} %get-tuple-element.21), channel_id=1, source_target_pairs={{0,2},{1,3},{2,0},{3,1},{4,6},{5,7},{6,4},{7,5},{8,10},{9,11},{10,... | collective-permute-start | bytes 245768 | tf_op jit(solution)/shard_map/ppermute | solution.py:22
  322.7 0.5 collective-permute-start.14
  323.1 3.7 %collective-permute-done.15 = f32[5,32,128]{2,1,0:T(8,128)S(1)} collective-permute-done((f32[5,32,128]{2,1,0:T(8,128)S(1)}, f32[5,32,128]{2,1,0:T(8,128)S(1)}, u32[]{:S(2)}, u32[]{:S(2)}) %collective-permute-start.15) | collective-permute-done | bytes 81952 | tf_op jit(solution)/shard_map/ppermute | solution.py:22
  326.8 1.0 collective-permute-done.14
  327.9 0.7 collective-permute-start.17
  328.6 3.3 collective-permute-start.18
  331.9 0.5 collective-permute-start.19
  332.4 0.9 collective-permute-done.17
  333.3 1.9 collective-permute-done.18
  335.2 2.9 collective-permute-done.19
  338.2 0.6 bitcast_dynamic-update-slice_fusion
  (28 shorter events, 0.2 us)
Async XLA Ops:
  6.5 256.9 %all-gather.2.cloned.1.call-start = ((), (), s32[]{:S(2)}) async-start(), calls=%async_computation.1 | async-start | bytes 7864320 | tf_op jit(solution)/shard_map/all_gather | solution.py:114
  10.1 1.4 copy-start.3
  95.3 81.6 %copy-start.1 = (bf16[512,4,384]{2,0,1:T(8,128)(2,1)}, bf16[512,4,384]{2,0,1:T(8,128)(2,1)S(1)}, u32[]{:S(2)}) copy-start(bf16[512,4,384]{2,0,1:T(8,128)(2,1)S(1)} %all_to_all.19) | copy-start | bytes 4718596
  95.3 82.9 %collective-permute-start.4 = (bf16[2048,384]{1,0:T(8,128)(2,1)S(1)}, bf16[2048,384]{1,0:T(8,128)(2,1)S(1)}, u32[]{:S(2)}, u32[]{:S(2)}) collective-permute-start(bf16[2048,384]{1,0:T(8,128)(2,1)S(1)} %bitcast.53), channel_id=1, source_target_pairs={{12,44},{13,45},{14,46},{15,47},{16,48},{17,49},{18,50},{19,51},{2... | collective-permute-start | bytes 4718600 | tf_op jit(solution)/shard_map/ppermute | solution.py:22
  101.4 34.1 %collective-permute-start = (bf16[512,384]{1,0:T(8,128)(2,1)}, bf16[512,384]{1,0:T(8,128)(2,1)}, u32[]{:S(2)}, u32[]{:S(2)}) collective-permute-start(bf16[512,384]{1,0:T(8,128)(2,1)} %get-tuple-element.12), channel_id=1, source_target_pairs={{108,143},{109,142},{110,141},{111,140},{112,147},{113,146},{114,1... | collective-permute-start | bytes 1179656 | tf_op jit(solution)/shard_map/ppermute | solution.py:22
  102.7 70.7 %collective-permute-start.1 = (bf16[512,384]{1,0:T(8,128)(2,1)}, bf16[512,384]{1,0:T(8,128)(2,1)}, u32[]{:S(2)}, u32[]{:S(2)}) collective-permute-start(bf16[512,384]{1,0:T(8,128)(2,1)} %get-tuple-element.11), channel_id=1, source_target_pairs={{108,142},{109,143},{110,140},{111,141},{112,146},{113,147},{114,1... | collective-permute-start | bytes 1179656 | tf_op jit(solution)/shard_map/ppermute | solution.py:22
  104.0 70.5 %collective-permute-start.2 = (bf16[512,384]{1,0:T(8,128)(2,1)}, bf16[512,384]{1,0:T(8,128)(2,1)}, u32[]{:S(2)}, u32[]{:S(2)}) collective-permute-start(bf16[512,384]{1,0:T(8,128)(2,1)} %get-tuple-element.13), channel_id=1, source_target_pairs={{108,141},{109,140},{110,143},{111,142},{112,145},{113,144},{114,1... | collective-permute-start | bytes 1179656 | tf_op jit(solution)/shard_map/ppermute | solution.py:22
  105.3 70.2 %collective-permute-start.3 = (bf16[512,384]{1,0:T(8,128)(2,1)}, bf16[512,384]{1,0:T(8,128)(2,1)S(1)}, u32[]{:S(2)}, u32[]{:S(2)}) collective-permute-start(bf16[512,384]{1,0:T(8,128)(2,1)} %get-tuple-element.10), channel_id=1, source_target_pairs={{108,140},{109,141},{110,142},{111,143},{112,144},{113,145},{114,1... | collective-permute-start | bytes 1179656 | tf_op jit(solution)/shard_map/ppermute | solution.py:22
  175.6 31.0 %collective-permute-start.9 = (bf16[2048,384]{1,0:T(8,128)(2,1)S(1)}, bf16[2048,384]{1,0:T(8,128)(2,1)}, u32[]{:S(2)}, u32[]{:S(2)}) collective-permute-start(bf16[2048,384]{1,0:T(8,128)(2,1)S(1)} %bitcast.54), channel_id=1, source_target_pairs={{0,16},{1,17},{2,18},{3,19},{4,20},{5,21},{6,22},{7,23},{8,24},{9,... | collective-permute-start | bytes 4718600 | tf_op jit(solution)/shard_map/ppermute | solution.py:22
  176.9 39.3 %collective-permute-start.6 = (bf16[2048,384]{1,0:T(8,128)(2,1)S(1)}, bf16[2048,384]{1,0:T(8,128)(2,1)}, u32[]{:S(2)}, u32[]{:S(2)}) collective-permute-start(bf16[2048,384]{1,0:T(8,128)(2,1)S(1)} %bitcast.55), channel_id=1, source_target_pairs={{0,8},{1,9},{2,10},{3,11},{4,12},{5,13},{6,14},{7,15},{8,16},{9,17... | collective-permute-start | bytes 4718600 | tf_op jit(solution)/shard_map/ppermute | solution.py:22
  179.6 36.6 %collective-permute-start.8 = (bf16[2048,384]{1,0:T(8,128)(2,1)}, bf16[2048,384]{1,0:T(8,128)(2,1)S(1)}, u32[]{:S(2)}, u32[]{:S(2)}) collective-permute-start(bf16[2048,384]{1,0:T(8,128)(2,1)} %broadcast_select_fusion.1), channel_id=1, source_target_pairs={{16,0},{17,1},{18,2},{19,3},{20,4},{21,5},{22,6},{23,7},{24,8},{25... | collective-permute-start | bytes 4718600 | tf_op jit(solution)/shard_map/ppermute | solution.py:22
  187.5 61.4 %collective-permute-start.5 = (bf16[2048,384]{1,0:T(8,128)(2,1)}, bf16[2048,384]{1,0:T(8,128)(2,1)}, u32[]{:S(2)}, u32[]{:S(2)}) collective-permute-start(bf16[2048,384]{1,0:T(8,128)(2,1)} %broadcast_select_fusion.1), channel_id=1, source_target_pairs={{24,0},{25,1},{26,2},{27,3},{28,4},{29,5},{30,6},{31,7},{56,32},{5... | collective-permute-start | bytes 4718600 | tf_op jit(solution)/shard_map/ppermute | solution.py:22
  191.6 60.8 %copy-start.2 = (bf16[512,4,384]{2,0,1:T(8,128)(2,1)S(1)}, bf16[512,4,384]{2,0,1:T(8,128)(2,1)}, u32[]{:S(2)}) copy-start(bf16[512,4,384]{2,0,1:T(8,128)(2,1)} %copy-done.1) | copy-start | bytes 4718596
  216.3 1.1 copy-start.4
  253.9 9.5 %collective-permute-start.7 = (bf16[2048,384]{1,0:T(8,128)(2,1)}, bf16[2048,384]{1,0:T(8,128)(2,1)}, u32[]{:S(2)}, u32[]{:S(2)}) collective-permute-start(bf16[2048,384]{1,0:T(8,128)(2,1)} %broadcast_select_fusion.4), channel_id=1, source_target_pairs={{0,4},{1,5},{2,6},{3,7},{4,0},{5,1},{6,2},{7,3},{8,12},{9,13},{10,... | collective-permute-start | bytes 4718600 | tf_op jit(solution)/shard_map/ppermute | solution.py:22
  255.6 31.3 %collective-permute-start.12 = (bf16[2048,384]{1,0:T(8,128)(2,1)}, bf16[2048,384]{1,0:T(8,128)(2,1)}, u32[]{:S(2)}, u32[]{:S(2)}) collective-permute-start(bf16[2048,384]{1,0:T(8,128)(2,1)} %bitcast.56), channel_id=1, source_target_pairs={{4,24},{5,25},{6,26},{7,27},{36,56},{37,57},{38,58},{39,59},{68,88... | collective-permute-start | bytes 4718600 | tf_op jit(solution)/shard_map/ppermute | solution.py:22
  256.9 30.0 %collective-permute-start.11 = (bf16[2048,384]{1,0:T(8,128)(2,1)}, bf16[2048,384]{1,0:T(8,128)(2,1)}, u32[]{:S(2)}, u32[]{:S(2)}) collective-permute-start(bf16[2048,384]{1,0:T(8,128)(2,1)} %broadcast_select_fusion.1), channel_id=1, source_target_pairs={{12,0},{13,1},{14,2},{15,3},{20,8},{21,9},{22,10},{23,11},{28,16},... | collective-permute-start | bytes 4718600 | tf_op jit(solution)/shard_map/ppermute | solution.py:22
  258.7 16.2 %collective-permute-start.10 = (bf16[2048,384]{1,0:T(8,128)(2,1)}, bf16[2048,384]{1,0:T(8,128)(2,1)}, u32[]{:S(2)}, u32[]{:S(2)}) collective-permute-start(bf16[2048,384]{1,0:T(8,128)(2,1)} %get-tuple-element.7), channel_id=1, source_target_pairs={{0,4},{1,5},{2,6},{3,7},{4,0},{5,1},{6,2},{7,3},{8,12},{9,13},{10,... | collective-permute-start | bytes 4718600 | tf_op jit(solution)/shard_map/ppermute | solution.py:22
  260.3 26.5 %collective-permute-start.13 = (bf16[2048,384]{1,0:T(8,128)(2,1)S(1)}, bf16[2048,384]{1,0:T(8,128)(2,1)}, u32[]{:S(2)}, u32[]{:S(2)}) collective-permute-start(bf16[2048,384]{1,0:T(8,128)(2,1)S(1)} %get-tuple-element.8), channel_id=1, source_target_pairs={{0,4},{1,5},{2,6},{3,7},{8,12},{9,13},{10,14},{11,15},{16,20},{17,... | collective-permute-start | bytes 4718600 | tf_op jit(solution)/shard_map/ppermute | solution.py:22
  263.4 7.7 %copy-start = (bf16[2048,1536]{1,0:T(8,128)(2,1)S(1)}, bf16[2048,1536]{1,0:T(8,128)(2,1)}, u32[]{:S(2)}) copy-start(bf16[2048,1536]{1,0:T(8,128)(2,1)} %all-gather.2.cloned.1.call-done) | copy-start | bytes 18874372
  293.0 30.1 %collective-permute-start.16 = (f32[5,32,128]{2,1,0:T(8,128)S(1)}, f32[5,32,128]{2,1,0:T(8,128)S(1)}, u32[]{:S(2)}, u32[]{:S(2)}) collective-permute-start(f32[5,32,128]{2,1,0:T(8,128)S(1)} %get-tuple-element.20), channel_id=1, source_target_pairs={{0,3},{1,2},{2,1},{3,0},{4,7},{5,6},{6,5},{7,4},{8,11},{9,10},{10,... | collective-permute-start | bytes 245768 | tf_op jit(solution)/shard_map/ppermute | solution.py:22
  293.4 33.4 %collective-permute-start.15 = (f32[5,32,128]{2,1,0:T(8,128)S(1)}, f32[5,32,128]{2,1,0:T(8,128)S(1)}, u32[]{:S(2)}, u32[]{:S(2)}) collective-permute-start(f32[5,32,128]{2,1,0:T(8,128)S(1)} %get-tuple-element.21), channel_id=1, source_target_pairs={{0,2},{1,3},{2,0},{3,1},{4,6},{5,7},{6,4},{7,5},{8,10},{9,11},{10,... | collective-permute-start | bytes 245768 | tf_op jit(solution)/shard_map/ppermute | solution.py:22
  322.7 5.2 %collective-permute-start.14 = (f32[5,32,128]{2,1,0:T(8,128)S(1)}, f32[5,32,128]{2,1,0:T(8,128)S(1)}, u32[]{:S(2)}, u32[]{:S(2)}) collective-permute-start(f32[5,32,128]{2,1,0:T(8,128)S(1)} %get-tuple-element.19), channel_id=1, source_target_pairs={{0,1},{1,0},{2,3},{3,2},{4,5},{5,4},{6,7},{7,6},{8,9},{9,8},{10,11... | collective-permute-start | bytes 245768 | tf_op jit(solution)/shard_map/ppermute | solution.py:22
  327.9 5.4 %collective-permute-start.17 = (f32[5,32,128]{2,1,0:T(8,128)S(1)}, f32[5,32,128]{2,1,0:T(8,128)S(1)}, u32[]{:S(2)}, u32[]{:S(2)}) collective-permute-start(f32[5,32,128]{2,1,0:T(8,128)S(1)} %get-tuple-element.6), channel_id=1, source_target_pairs={{0,1},{1,0},{2,3},{3,2},{4,5},{5,4},{6,7},{7,6},{8,9},{9,8},{10,11... | collective-permute-start | bytes 245768 | tf_op jit(solution)/shard_map/ppermute | solution.py:22
  328.6 6.6 %collective-permute-start.18 = (f32[5,32,128]{2,1,0:T(8,128)S(1)}, f32[5,32,128]{2,1,0:T(8,128)S(1)}, u32[]{:S(2)}, u32[]{:S(2)}) collective-permute-start(f32[5,32,128]{2,1,0:T(8,128)S(1)} %get-tuple-element.6), channel_id=1, source_target_pairs={{0,2},{1,3},{2,0},{3,1},{4,6},{5,7},{6,4},{7,5},{8,10},{9,11},{10,... | collective-permute-start | bytes 245768 | tf_op jit(solution)/shard_map/ppermute | solution.py:22
  331.9 6.2 %collective-permute-start.19 = (f32[5,32,128]{2,1,0:T(8,128)S(1)}, f32[5,32,128]{2,1,0:T(8,128)S(1)}, u32[]{:S(2)}, u32[]{:S(2)}) collective-permute-start(f32[5,32,128]{2,1,0:T(8,128)S(1)} %get-tuple-element.6), channel_id=1, source_target_pairs={{0,3},{1,2},{2,1},{3,0},{4,7},{5,6},{6,5},{7,4},{8,11},{9,10},{10,... | collective-permute-start | bytes 245768 | tf_op jit(solution)/shard_map/ppermute | solution.py:22
  335.2 2.9 copy-start.5
Sparse Core Ops, SparseCore 0:
  10.2 137.5 all-gather.1
